TPU v7x, 512 devices: a whole 4x8x8 slice. The times are simulated.
512 devices in a mesh: blk: 128 (over z, y, core), pair: 4 (over x).
Axes of the slice: x: 4, y: 8, z: 8, core: 2. Of those that a mesh axis runs over, the one named last changes fastest.
Arguments:
- features: bfloat16 [557, 786432], P(None, ('blk', 'pair')), may hold values from -6 to 6
- daylit_list: int32 [786432], P(('blk', 'pair')), may hold values from 0 to 1535, as said below
- daylit_count: int32 [512], P(('blk', 'pair')), may hold values from 0 to 1536
- in_weight: bfloat16 [557, 512], replicated, may hold values from -0.25 to 0.25
- in_bias: float32 [512], replicated, may hold values from -3 to 3
- mid_weight: bfloat16 [2, 512, 512], replicated, may hold values from -0.25 to 0.25
- mid_bias: float32 [2, 512], replicated, may hold values from -3 to 3
- out_weight: bfloat16 [368, 512], replicated, may hold values from -0.25 to 0.25
- out_bias: float32 [368], replicated, may hold values from -3 to 3
Outputs:
- heating: bfloat16 [368, 786432], P(None, ('blk', 'pair'))
Inputs may be any that keep to these rules, and one draw needn't show every extreme that they name: `daylit_list`: the first daylit_count[d] of block d's 1536 entries are the local indices of its daylit columns in increasing order; the remaining entries are 0. The column with local index j of block (blk, pair) and the one with the same j of block (blk, (pair + 2) mod 4) lie half a globe apart, and exactly one of the two is daylit.
All inputs are finite; a program needn't handle non-finite values.
Results may differ from a plain program's by a relative error of at most 0.0052.
Values may be sent and summed in bfloat16 or wider, within the bound.
A program may use at most 64 MiB of HBM per device.

v0:
```python
import jax
import jax.numpy as jnp
from jax import lax
from jax.experimental import pallas as pl
from jax.experimental.pallas import tpu as pltpu
from jax.sharding import PartitionSpec as P

FEAT, HID, OUT = 557, 512, 368
LANES = 384
NX, NZ, NY, NC, NK = 4, 8, 8, 2, 3
BLOCK = NZ * NY * NC * NK
ROWS = NZ * NY
COLS = NX * BLOCK
OFFSETS = (1, 3, 2, 0)
RING = (4, 3, 5, 2, 6, 1, 7)
VMEM = 62 * 1024 * 1024
LOADED = (5, 6, 9, 10)
BF16, F32 = jnp.bfloat16, jnp.float32
MESH = pl.DeviceIdType.MESH


def nt(a, b):
    return lax.dot_general(a, b, (((1,), (1,)), ((), ())), preferred_element_type=F32)


def leaky(t):
    return jnp.maximum(t, 0.15 * t)


def selector(rows, cols, column_of_row):
    r = lax.broadcasted_iota(jnp.int32, (rows, cols), 0)
    c = lax.broadcasted_iota(jnp.int32, (rows, cols), 1)
    return jnp.where(c == column_of_row(r), 1.0, 0.0).astype(BF16)


def column(row):
    return jnp.transpose(jnp.broadcast_to(row, (128, row.shape[1])))


def kernel(
    count_ref, list_ref, feat_ref, w0_ref, b0_ref, wm_ref, bm_ref, wo_ref, bo_ref, out_ref,
    list_v, f_v, w0_v, b0_v, wm_v, bm_v, wo_v, bo_v, day_v, w0t_v, pick_v, place_v, sx, rx, zs, zr, ys, yr, t_v,
    load_sem, sx_sem, rx_sem, zs_sem, zr_sem, ys_sem, yr_sem, t_sem,
):
    x = lax.axis_index("pair")
    blk = lax.axis_index("blk")
    z, y, c = blk // (NY * NC), (blk // NC) % NY, blk % NC

    def blk_of(zz, yy, cc):
        return (zz * NY + yy) * NC + cc

    sectors = [lax.rem(x + off, NX) for off in OFFSETS]

    def features_of(i):
        return (
            feat_ref.at[:, pl.ds(pl.multiple_of(sectors[i] * BLOCK, 128), BLOCK)],
            f_v.at[i],
        )

    loads = [
        pltpu.make_async_copy(src, dst, load_sem.at[n])
        for n, (src, dst) in enumerate(
            (
                (list_ref, list_v),
                (b0_ref, b0_v),
                (bm_ref, bm_v),
                (bo_ref, bo_v),
                (w0_ref, w0_v),
                features_of(0),
                features_of(1),
                (wm_ref, wm_v),
                (wo_ref, wo_v.at[pl.ds(0, OUT)]),
                features_of(2),
                features_of(3),
            )
        )
    ]
    for load in loads:
        load.start()

    barrier = pltpu.get_barrier_semaphore()
    peers = []
    for a in sectors:
        peers.append((blk_of(z, y, 1 - c), a))
    for a in sectors[:3]:
        peers.append((blk, a))
    for d in RING:
        peers.append((blk_of(lax.rem(z + d, NZ), y, c), x))
    for d in RING:
        peers.append((blk_of(z, lax.rem(y + d, NY), c), x))
    for peer in peers:
        pl.semaphore_signal(barrier, inc=1, device_id=peer, device_id_type=MESH)

    pick_v[...] = selector(
        BLOCK, BLOCK, lambda r: (r % NK) * 128 + ((r // NK) & 1) * ROWS + r // (NK * NC)
    )
    wo_v[pl.ds(OUT, LANES - OUT), :] = jnp.zeros((LANES - OUT, HID), BF16)

    for load in loads[:4]:
        load.wait()
    entries = list_v[...].reshape(1, COLS)
    usable = lax.broadcasted_iota(jnp.int32, (1, COLS), 1) < count_ref[0]
    high = jnp.where(usable, entries >> 7, -1)
    high = jnp.broadcast_to(high, (16, COLS)) == lax.broadcasted_iota(jnp.int32, (16, COLS), 0)
    low = jnp.broadcast_to(entries & 127, (128, COLS)) == lax.broadcasted_iota(
        jnp.int32, (128, COLS), 0
    )
    day_v[...] = nt(
        jnp.where(high, 1.0, 0.0).astype(BF16), jnp.where(low, 1.0, 0.0).astype(BF16)
    )
    biases = [column(b0_v[...].reshape(1, HID))]
    biases += [column(bm_v[pl.ds(n, 1), :]) for n in range(2)]
    bias_out = jnp.concatenate([bo_v[...].reshape(1, OUT), jnp.zeros((1, LANES - OUT), F32)], axis=1)
    biases.append(column(bias_out))
    first_half = jnp.where(x < NX // 2, 1.0, 0.0)

    loads[4].wait()
    eye = selector(256, 256, lambda r: r)
    for lo in range(0, HID, 256):
        w0t_v[pl.ds(lo, 256), :] = nt(eye, w0_v[:, pl.ds(lo, 256)]).astype(BF16)

    def network(half, first, count):
        picked, days = [], []
        lanes = pl.ds(first * 128, count * 128)
        for i in (2 * half, 2 * half + 1):
            if first == 0:
                loads[LOADED[i]].wait()
            part = jnp.dot(f_v[i], pick_v[:, lanes], preferred_element_type=F32)
            picked.append(part.astype(BF16))
            day = jnp.concatenate(
                [day_v[pl.ds(sectors[i] * NK + t, 1), :] for t in range(NK)], axis=1
            )
            day = jnp.broadcast_to(jnp.where(day > 0.5, 1.0, 0.0), (16, BLOCK)).astype(BF16)
            days.append(jnp.dot(day, pick_v[:, lanes], preferred_element_type=F32)[:1])
        h, day = jnp.concatenate(picked, axis=1), jnp.concatenate(days, axis=1)
        tiled = [jnp.concatenate([b] * (2 * count), axis=1) for b in biases]
        h = jnp.dot(w0t_v[...], h, preferred_element_type=F32)
        h = leaky(h + tiled[0]).astype(BF16)
        if half == 0 and first == 0:
            loads[7].wait()
        for layer in range(2):
            h = jnp.dot(wm_v[layer], h, preferred_element_type=F32)
            h = leaky(h + tiled[1 + layer]).astype(BF16)
        if half == 0 and first == 0:
            loads[8].wait()
        v = jnp.dot(wo_v[...], h, preferred_element_type=F32) + tiled[3]
        feat = lax.broadcasted_iota(jnp.int32, v.shape, 0)
        v = (jnp.where(feat == OUT, first_half, v) * day).astype(BF16)
        for n in range(2 * count):
            rows = nt(eye[:128, :128], v[:, n * 128 : (n + 1) * 128]).astype(BF16)
            sx[2 * half + n // count, first + n % count] = rows.reshape(NC, ROWS, LANES)

    def send(src, dst, send_sem, recv_sem, device):
        pltpu.make_async_remote_copy(
            src_ref=src,
            dst_ref=dst,
            send_sem=send_sem,
            recv_sem=recv_sem,
            device_id=device,
            device_id_type=MESH,
        ).start()

    def send_x(half, k):
        for i in (2 * half, 2 * half + 1):
            for cc in range(NC) if i < 3 else (1 - c,):
                dst = rx.at[half, k, 2 * (i % 2) + c]
                device = (blk_of(z, y, cc), sectors[i])
                send(sx.at[i, k, cc], dst, sx_sem.at[0], rx_sem.at[half, k], device)
        if half == 1:
            rx[1, k, pl.ds(2 + c, 1)] = sx[3, k, pl.ds(c, 1)]

    def wait_for(view, sem):
        pltpu.make_async_copy(view, view, sem).wait()

    def parts_of(half, k):
        return ((0, 256), (256, 128)) if (half, k) == (1, NK - 1) else ((0, LANES),)

    def stage_x(half, k):
        wait_for(rx.at[half, k, pl.ds(0, 4 - half)], rx_sem.at[half, k])
        sums = [
            (rx[half, k, cc].astype(F32) + rx[half, k, 2 + cc].astype(F32)).reshape(NZ, NY, LANES)
            for cc in range(NC)
        ]
        zs[half, k] = jnp.concatenate(sums, axis=1).astype(BF16)
        for p, (lo, width) in enumerate(parts_of(half, k)):
            lanes = pl.ds(lo, width)
            for d in RING:
                zz = lax.rem(z + d, NZ)
                src, dst = zs.at[half, k, zz, :, lanes], zr.at[half, k, z, :, lanes]
                send(src, dst, zs_sem.at[0], zr_sem.at[half, k, p], (blk_of(zz, y, c), x))
        zr[half, k, pl.ds(z, 1)] = zs[half, k, pl.ds(z, 1)]

    def stage_z(half, k):
        for p, (lo, width) in enumerate(parts_of(half, k)):
            lanes = pl.ds(lo, width)
            wait_for(zr.at[half, k, pl.ds(0, NZ - 1), :, lanes], zr_sem.at[half, k, p])
            rows = zr[half, k, :, :, lanes].reshape(128, width)
            turned = jnp.dot(turn, rows, preferred_element_type=F32)
            ys[half, k, :, :, lanes] = turned.astype(BF16).reshape(NY, 16, width)
            for d in RING:
                yy = lax.rem(y + d, NY)
                src, dst = ys.at[half, k, yy, :, lanes], yr.at[half, k, y, :, lanes]
                send(src, dst, ys_sem.at[0], yr_sem.at[half, k, p], (blk_of(z, yy, c), x))
        yr[half, k, pl.ds(y, 1)] = ys[half, k, pl.ds(y, 1)]

    def stage_y(half):
        near = lax.rem(x + 1 + half, 2)
        total = 0.0
        for k in range(NK):
            place = place_v[pl.ds(k * 128, 128), :]
            for p, (lo, width) in enumerate(parts_of(half, k)):
                lanes = pl.ds(lo, width)
                wait_for(yr.at[half, k, pl.ds(0, NY - 1), :, lanes], yr_sem.at[half, k, p])
                rows = yr[half, k, :, :, lanes].reshape(128, width)
                feats = [
                    nt(eye[:128, :128], rows[:, n : n + 128]).astype(BF16)
                    for n in range(0, width, 128)
                ]
                part = jnp.dot(
                    jnp.concatenate(feats, axis=0), place, preferred_element_type=F32
                )
                if k < NK - 1:
                    total = total + part
                    continue
                t_v[half, lanes] = (total[lo : lo + width] + part).astype(BF16)
                pltpu.make_async_copy(
                    t_v.at[half, lanes], out_ref.at[near, lanes], t_sem.at[half]
                ).start()

    chunks = [(half, k) for half in range(2) for k in range(NK)]
    network(0, 0, 1)
    pl.semaphore_wait(barrier, len(peers))
    send_x(0, 0)
    network(0, 1, 2)
    send_x(0, 1)
    send_x(0, 2)
    turn = selector(128, 128, lambda r: (r & 15) * 8 + (r >> 4))
    network(1, 0, 1)
    send_x(1, 0)
    stage_x(0, 0)
    network(1, 1, 2)
    send_x(1, 1)
    send_x(1, 2)
    place_v[...] = selector(
        BLOCK,
        BLOCK,
        lambda r: (((r >> 1) & 7) * 16 + ((r >> 4) & 7) * 2 + (r & 1)) * NK + (r >> 7),
    )
    for t in range(1, len(chunks) + 1):
        if t < len(chunks):
            stage_x(*chunks[t])
        stage_z(*chunks[t - 1])
    for half in range(2):
        stage_y(half)

    wait_for(sx.at[pl.ds(0, 3)], sx_sem.at[0])
    wait_for(sx.at[3, :, 0], sx_sem.at[0])
    wait_for(zs.at[:, :, pl.ds(0, NZ - 1)], zs_sem.at[0])
    wait_for(ys.at[:, :, pl.ds(0, NY - 1)], ys_sem.at[0])
    for half in range(2):
        wait_for(t_v.at[half], t_sem.at[half])


def spread(t_ref, out_ref, t_v, o_v, t_sem, o_sem):
    pieces = [(n, pl.ds(b * 128, 128)) for n in range(2) for b in range(NK)]
    loads = [
        pltpu.make_async_copy(t_ref.at[n, :, lanes], t_v.at[m], t_sem.at[m])
        for m, (n, lanes) in enumerate(pieces)
    ]
    for load in loads:
        load.start()
    stores = []
    for m, (n, _) in enumerate(pieces):
        loads[m].wait()
        values = t_v[m].astype(F32)
        flag = values[OUT : OUT + 1]
        for far, weight in enumerate((flag, 1.0 - flag)):
            slot = m + 6 * far
            o_v[slot] = (values[:OUT] * weight).astype(BF16)
            store = pltpu.make_async_copy(
                o_v.at[slot], out_ref.at[:, pl.ds(slot * 128, 128)], o_sem.at[slot]
            )
            store.start()
            stores.append(store)
    for store in stores:
        store.wait()


def shards(
    features, daylit_list, daylit_count, in_weight, in_bias, mid_weight, mid_bias, out_weight, out_bias
):
    hbm = pl.BlockSpec(memory_space=pltpu.HBM)
    dma = pltpu.SemaphoreType.DMA
    halves = pl.pallas_call(
        kernel,
        out_shape=jax.ShapeDtypeStruct((2, LANES, BLOCK), BF16),
        in_specs=[pl.BlockSpec(memory_space=pltpu.SMEM)] + [hbm] * 8,
        out_specs=hbm,
        scratch_shapes=[
            pltpu.VMEM((COLS,), jnp.int32),
            pltpu.VMEM((4, FEAT, BLOCK), BF16),
            pltpu.VMEM((FEAT, HID), BF16),
            pltpu.VMEM((HID,), F32),
            pltpu.VMEM((2, HID, HID), BF16),
            pltpu.VMEM((2, HID), F32),
            pltpu.VMEM((LANES, HID), BF16),
            pltpu.VMEM((OUT,), F32),
            pltpu.VMEM((16, 128), F32),
            pltpu.VMEM((HID, FEAT), BF16),
            pltpu.VMEM((BLOCK, BLOCK), BF16),
            pltpu.VMEM((BLOCK, BLOCK), BF16),
            pltpu.VMEM((NX, NK, NC, ROWS, LANES), BF16),
            pltpu.VMEM((2, NK, 4, ROWS, LANES), BF16),
            pltpu.VMEM((2, NK, NZ, 16, LANES), BF16),
            pltpu.VMEM((2, NK, NZ, 16, LANES), BF16),
            pltpu.VMEM((2, NK, NY, 16, LANES), BF16),
            pltpu.VMEM((2, NK, NY, 16, LANES), BF16),
            pltpu.VMEM((2, LANES, BLOCK), BF16),
            dma((11,)),
            dma((1,)),
            dma((2, NK)),
            dma((1,)),
            dma((2, NK, 2)),
            dma((1,)),
            dma((2, NK, 2)),
            dma((2,)),
        ],
        compiler_params=pltpu.CompilerParams(
            collective_id=0, has_side_effects=True, vmem_limit_bytes=VMEM
        ),
    )(
        daylit_count,
        daylit_list,
        features,
        in_weight,
        in_bias,
        mid_weight,
        mid_bias,
        out_weight,
        out_bias,
    )
    return pl.pallas_call(
        spread,
        out_shape=jax.ShapeDtypeStruct((OUT, COLS), BF16),
        in_specs=[hbm],
        out_specs=hbm,
        scratch_shapes=[
            pltpu.VMEM((6, LANES, 128), BF16),
            pltpu.VMEM((12, OUT, 128), BF16),
            dma((6,)),
            dma((12,)),
        ],
        compiler_params=pltpu.CompilerParams(vmem_limit_bytes=VMEM),
    )(halves)


def solution(mesh):
    in_specs = (
        P(None, ("blk", "pair")),
        P(("blk", "pair")),
        P(("blk", "pair")),
        P(),
        P(),
        P(),
        P(),
        P(),
        P(),
    )
    out_specs = P(None, ("blk", "pair"))
    return jax.shard_map(shards, mesh=mesh, in_specs=in_specs, out_specs=out_specs, check_vma=False)
```

profile of v0, /device:TPU:1, one launch (start us, length us, event | category | flops | bytes accessed | tf_op | source)
XLA Modules:
  0.0 48.1 jit_solution(8660182804859501008)
XLA Ops:
  0.7 45.4 %shard_map.91.t_ref = bf16[2,384,384]{2,1,0:T(8,128)(2,1)} custom-call(s32[1]{0:T(128)S(6)} %copy.10.count_ref, s32[1536]{0:T(1024)} %list_ref.1, bf16[557,1536]{1,0:T(8,128)(2,1)} %feat_ref.1, bf16[557,512]{1,0:T(8,128)(2,1)} %w0_ref.1, f32[512]{0:T(512)} %b0_ref.1, bf16[2,512,512]{2,1,0:T(8,128)(2,1)} %wm_ref.1, f32[2,512]{1,0:T(2,128)} %bm_ref.1, ...), custom_call_target="tpu_custom_call" | custom-call | tf_op jit(solution)/shard_map/pallas_call | solution.py:294
  46.1 2.0 %shard_map.92 = bf16[368,1536]{1,0:T(8,128)(2,1)} custom-call(bf16[2,384,384]{2,1,0:T(8,128)(2,1)} %shard_map.91.t_ref), custom_call_target="tpu_custom_call" | custom-call | tf_op jit(solution)/shard_map/pallas_call | solution.py:342
where the time goes:
time: 48.3 us; the launch traced here: 48.1 us
  Pallas kernels  47.5 us (98%)
  between operations  0.66 us (1%)
    pallas_call x1, Pallas kernels, shards(): pl.pallas_call(kernel, out_shape=jax.ShapeDtypeStruct((2, LANES, BLOCK),...  45.4 us
    pallas_call x1, Pallas kernels, shards(): pl.pallas_call(spread, out_shape=jax.ShapeDtypeStruct((OUT, COLS), BF16),...  2.05 us

commit v1 on v0

--- a/solution.py
+++ b/solution.py
@@ -27,10 +27,10 @@
     return jnp.maximum(t, 0.15 * t)
 
 
-def selector(rows, cols, column_of_row):
+def selector(rows, cols, row_of_column):
     r = lax.broadcasted_iota(jnp.int32, (rows, cols), 0)
-    c = lax.broadcasted_iota(jnp.int32, (rows, cols), 1)
-    return jnp.where(c == column_of_row(r), 1.0, 0.0).astype(BF16)
+    wanted = row_of_column(lax.broadcasted_iota(jnp.int32, (1, cols), 1))
+    return jnp.where(r == wanted, 1.0, 0.0).astype(BF16)
 
 
 def column(row):
@@ -79,21 +79,22 @@
         load.start()
 
     barrier = pltpu.get_barrier_semaphore()
-    peers = []
-    for a in sectors:
-        peers.append((blk_of(z, y, 1 - c), a))
-    for a in sectors[:3]:
-        peers.append((blk, a))
-    for d in RING:
-        peers.append((blk_of(lax.rem(z + d, NZ), y, c), x))
-    for d in RING:
-        peers.append((blk_of(z, lax.rem(y + d, NY), c), x))
+    other = blk_of(z, y, 1 - c)
+    cores = (blk, other)
+    along_z = [blk_of(lax.rem(z + d, NZ), y, c) for d in range(NZ)]
+    along_y = [blk_of(z, lax.rem(y + d, NY), c) for d in range(NY)]
+    peers = [(other, a) for a in sectors]
+    peers += [(blk, a) for a in sectors[:3]]
+    peers += [(along_z[d], x) for d in RING]
+    peers += [(along_y[d], x) for d in RING]
     for peer in peers:
         pl.semaphore_signal(barrier, inc=1, device_id=peer, device_id_type=MESH)
 
-    pick_v[...] = selector(
-        BLOCK, BLOCK, lambda r: (r % NK) * 128 + ((r // NK) & 1) * ROWS + r // (NK * NC)
-    )
+    def picked_from(q):
+        zz, yy = ((q >> 3) + z) & 7, (q + y) & 7
+        return (zz * NY + yy) * (NC * NK) + (((q >> 6) & 1) ^ c) * NK + (q >> 7)
+
+    pick_v[...] = selector(BLOCK, BLOCK, picked_from)
     wo_v[pl.ds(OUT, LANES - OUT), :] = jnp.zeros((LANES - OUT, HID), BF16)
 
     for load in loads[:4]:
@@ -162,70 +163,57 @@
 
     def send_x(half, k):
         for i in (2 * half, 2 * half + 1):
-            for cc in range(NC) if i < 3 else (1 - c,):
-                dst = rx.at[half, k, 2 * (i % 2) + c]
-                device = (blk_of(z, y, cc), sectors[i])
-                send(sx.at[i, k, cc], dst, sx_sem.at[0], rx_sem.at[half, k], device)
-        if half == 1:
-            rx[1, k, pl.ds(2 + c, 1)] = sx[3, k, pl.ds(c, 1)]
+            for r in range(NC) if i < 3 else (1,):
+                dst = rx.at[half, k, 2 * (i % 2) + r]
+                device = (cores[r], sectors[i])
+                send(sx.at[i, k, r], dst, sx_sem.at[0], rx_sem.at[half, k], device)
 
     def wait_for(view, sem):
         pltpu.make_async_copy(view, view, sem).wait()
 
-    def parts_of(half, k):
-        return ((0, 256), (256, 128)) if (half, k) == (1, NK - 1) else ((0, LANES),)
-
     def stage_x(half, k):
-        wait_for(rx.at[half, k, pl.ds(0, 4 - half)], rx_sem.at[half, k])
-        sums = [
-            (rx[half, k, cc].astype(F32) + rx[half, k, 2 + cc].astype(F32)).reshape(NZ, NY, LANES)
-            for cc in range(NC)
-        ]
-        zs[half, k] = jnp.concatenate(sums, axis=1).astype(BF16)
-        for p, (lo, width) in enumerate(parts_of(half, k)):
-            lanes = pl.ds(lo, width)
-            for d in RING:
-                zz = lax.rem(z + d, NZ)
-                src, dst = zs.at[half, k, zz, :, lanes], zr.at[half, k, z, :, lanes]
-                send(src, dst, zs_sem.at[0], zr_sem.at[half, k, p], (blk_of(zz, y, c), x))
-        zr[half, k, pl.ds(z, 1)] = zs[half, k, pl.ds(z, 1)]
+        slots = (0, 1, 2, 3) if half == 0 else (0, 1, 3)
+        wait_for(rx.at[half, k, pl.ds(0, len(slots))], rx_sem.at[half, k])
+        sums = []
+        for r in range(NC):
+            near = sx[3, k, 0] if half == 1 and r == 0 else rx[half, k, 2 + r]
+            total = rx[half, k, r].astype(F32) + near.astype(F32)
+            sums.append(total.reshape(NZ, NY, LANES))
+        merged = jnp.concatenate(sums, axis=1).astype(BF16)
+        zs[half, k] = merged
+        for d in RING:
+            dst = zr.at[half, k, d]
+            send(zs.at[half, k, d], dst, zs_sem.at[0], zr_sem.at[half, k], (along_z[d], x))
+        zr[half, k, 0] = merged[0]
 
     def stage_z(half, k):
-        for p, (lo, width) in enumerate(parts_of(half, k)):
-            lanes = pl.ds(lo, width)
-            wait_for(zr.at[half, k, pl.ds(0, NZ - 1), :, lanes], zr_sem.at[half, k, p])
-            rows = zr[half, k, :, :, lanes].reshape(128, width)
-            turned = jnp.dot(turn, rows, preferred_element_type=F32)
-            ys[half, k, :, :, lanes] = turned.astype(BF16).reshape(NY, 16, width)
-            for d in RING:
-                yy = lax.rem(y + d, NY)
-                src, dst = ys.at[half, k, yy, :, lanes], yr.at[half, k, y, :, lanes]
-                send(src, dst, ys_sem.at[0], yr_sem.at[half, k, p], (blk_of(z, yy, c), x))
-        yr[half, k, pl.ds(y, 1)] = ys[half, k, pl.ds(y, 1)]
+        wait_for(zr.at[half, k, pl.ds(1, NZ - 1)], zr_sem.at[half, k])
+        rows = zr[half, k].reshape(128, LANES)
+        turned = jnp.dot(turn, rows, preferred_element_type=F32)
+        turned = turned.astype(BF16).reshape(NY, 16, LANES)
+        ys[half, k] = turned
+        for e in RING:
+            dst = yr.at[half, k, e]
+            send(ys.at[half, k, e], dst, ys_sem.at[0], yr_sem.at[half, k], (along_y[e], x))
+        yr[half, k, 0] = turned[0]
 
     def stage_y(half):
         near = lax.rem(x + 1 + half, 2)
         total = 0.0
         for k in range(NK):
-            place = place_v[pl.ds(k * 128, 128), :]
-            for p, (lo, width) in enumerate(parts_of(half, k)):
-                lanes = pl.ds(lo, width)
-                wait_for(yr.at[half, k, pl.ds(0, NY - 1), :, lanes], yr_sem.at[half, k, p])
-                rows = yr[half, k, :, :, lanes].reshape(128, width)
-                feats = [
-                    nt(eye[:128, :128], rows[:, n : n + 128]).astype(BF16)
-                    for n in range(0, width, 128)
-                ]
-                part = jnp.dot(
-                    jnp.concatenate(feats, axis=0), place, preferred_element_type=F32
-                )
-                if k < NK - 1:
-                    total = total + part
-                    continue
-                t_v[half, lanes] = (total[lo : lo + width] + part).astype(BF16)
-                pltpu.make_async_copy(
-                    t_v.at[half, lanes], out_ref.at[near, lanes], t_sem.at[half]
-                ).start()
+            wait_for(yr.at[half, k, pl.ds(1, NY - 1)], yr_sem.at[half, k])
+            rows = yr[half, k].reshape(128, LANES)
+            feats = [
+                nt(eye[:128, :128], rows[:, n : n + 128]).astype(BF16)
+                for n in range(0, LANES, 128)
+            ]
+            total = total + jnp.dot(
+                jnp.concatenate(feats, axis=0),
+                place_v[pl.ds(k * 128, 128), :],
+                preferred_element_type=F32,
+            )
+        t_v[half] = total.astype(BF16)
+        pltpu.make_async_copy(t_v.at[half], out_ref.at[near], t_sem.at[half]).start()
 
     chunks = [(half, k) for half in range(2) for k in range(NK)]
     network(0, 0, 1)
@@ -234,18 +222,19 @@
     network(0, 1, 2)
     send_x(0, 1)
     send_x(0, 2)
-    turn = selector(128, 128, lambda r: (r & 15) * 8 + (r >> 4))
+    turn = selector(128, 128, lambda q: (q & 7) * 16 + (q >> 3))
     network(1, 0, 1)
     send_x(1, 0)
     stage_x(0, 0)
     network(1, 1, 2)
     send_x(1, 1)
     send_x(1, 2)
-    place_v[...] = selector(
-        BLOCK,
-        BLOCK,
-        lambda r: (((r >> 1) & 7) * 16 + ((r >> 4) & 7) * 2 + (r & 1)) * NK + (r >> 7),
-    )
+    def placed_from(q):
+        source = (q * 21846) >> 16
+        d, e = (z - (source >> 4)) & 7, (y - (source >> 1)) & 7
+        return (q - source * NK) * 128 + e * 16 + d * 2 + ((source & 1) ^ c)
+
+    place_v[...] = selector(BLOCK, BLOCK, placed_from)
     for t in range(1, len(chunks) + 1):
         if t < len(chunks):
             stage_x(*chunks[t])
@@ -254,9 +243,9 @@
         stage_y(half)
 
     wait_for(sx.at[pl.ds(0, 3)], sx_sem.at[0])
-    wait_for(sx.at[3, :, 0], sx_sem.at[0])
-    wait_for(zs.at[:, :, pl.ds(0, NZ - 1)], zs_sem.at[0])
-    wait_for(ys.at[:, :, pl.ds(0, NY - 1)], ys_sem.at[0])
+    wait_for(sx.at[3, :, 1], sx_sem.at[0])
+    wait_for(zs.at[:, :, pl.ds(1, NZ - 1)], zs_sem.at[0])
+    wait_for(ys.at[:, :, pl.ds(1, NY - 1)], ys_sem.at[0])
     for half in range(2):
         wait_for(t_v.at[half], t_sem.at[half])
 
@@ -320,9 +309,9 @@
             dma((1,)),
             dma((2, NK)),
             dma((1,)),
-            dma((2, NK, 2)),
+            dma((2, NK)),
             dma((1,)),
-            dma((2, NK, 2)),
+            dma((2, NK)),
             dma((2,)),
         ],
         compiler_params=pltpu.CompilerParams(

time: 48.3 us -> 47 us (0.973)
  Pallas kernels: 47.5 us -> 46.1 us
    pallas_call x1, Pallas kernels: 45.4 us -> 44.1 us  [shards(): pl.pallas_call(kernel, out_shape=jax.ShapeDtypeStruct((2, LANES, BLOCK),...]
where the time goes in v1:
time: 47 us; the launch traced here: 46.8 us
  Pallas kernels  46.1 us (98%)
  between operations  0.66 us (1%)
    pallas_call x1, Pallas kernels, shards(): pl.pallas_call(kernel, out_shape=jax.ShapeDtypeStruct((2, LANES, BLOCK),...  44.1 us
    pallas_call x1, Pallas kernels, shards(): pl.pallas_call(spread, out_shape=jax.ShapeDtypeStruct((OUT, COLS), BF16),...  2.05 us

profile of v1, /device:TPU:1, one launch (start us, length us, event | category | flops | bytes accessed | tf_op | source)
XLA Modules:
  0.0 46.8 jit_solution(6936845600319592637)
XLA Ops:
  0.7 44.1 %shard_map.91.t_ref = bf16[2,384,384]{2,1,0:T(8,128)(2,1)} custom-call(s32[1]{0:T(128)S(6)} %copy.10.count_ref, s32[1536]{0:T(1024)} %list_ref.1, bf16[557,1536]{1,0:T(8,128)(2,1)} %feat_ref.1, bf16[557,512]{1,0:T(8,128)(2,1)} %w0_ref.1, f32[512]{0:T(512)} %b0_ref.1, bf16[2,512,512]{2,1,0:T(8,128)(2,1)} %wm_ref.1, f32[2,512]{1,0:T(2,128)} %bm_ref.1, ...), custom_call_target="tpu_custom_call" | custom-call | tf_op jit(solution)/shard_map/pallas_call | solution.py:283
  44.7 2.0 %shard_map.92 = bf16[368,1536]{1,0:T(8,128)(2,1)} custom-call(bf16[2,384,384]{2,1,0:T(8,128)(2,1)} %shard_map.91.t_ref), custom_call_target="tpu_custom_call" | custom-call | tf_op jit(solution)/shard_map/pallas_call | solution.py:331

commit v2 on v1

--- a/solution.py
+++ b/solution.py
@@ -75,8 +75,8 @@
             )
         )
     ]
-    for load in loads:
-        load.start()
+    for n in (4, 5, 6, 0, 1, 2, 3, 7, 8, 9, 10):
+        loads[n].start()
 
     barrier = pltpu.get_barrier_semaphore()
     other = blk_of(z, y, 1 - c)
@@ -87,9 +87,6 @@
     peers += [(blk, a) for a in sectors[:3]]
     peers += [(along_z[d], x) for d in RING]
     peers += [(along_y[d], x) for d in RING]
-    for peer in peers:
-        pl.semaphore_signal(barrier, inc=1, device_id=peer, device_id_type=MESH)
-
     def picked_from(q):
         zz, yy = ((q >> 3) + z) & 7, (q + y) & 7
         return (zz * NY + yy) * (NC * NK) + (((q >> 6) & 1) ^ c) * NK + (q >> 7)
@@ -97,8 +94,14 @@
     pick_v[...] = selector(BLOCK, BLOCK, picked_from)
     wo_v[pl.ds(OUT, LANES - OUT), :] = jnp.zeros((LANES - OUT, HID), BF16)
 
-    for load in loads[:4]:
+    eye = selector(256, 256, lambda r: r)
+    turn = selector(128, 128, lambda q: (q & 7) * 16 + (q >> 3))
+
+    for load in loads[:7]:
         load.wait()
+    for peer in peers:
+        pl.semaphore_signal(barrier, inc=1, device_id=peer, device_id_type=MESH)
+
     entries = list_v[...].reshape(1, COLS)
     usable = lax.broadcasted_iota(jnp.int32, (1, COLS), 1) < count_ref[0]
     high = jnp.where(usable, entries >> 7, -1)
@@ -115,8 +118,6 @@
     biases.append(column(bias_out))
     first_half = jnp.where(x < NX // 2, 1.0, 0.0)
 
-    loads[4].wait()
-    eye = selector(256, 256, lambda r: r)
     for lo in range(0, HID, 256):
         w0t_v[pl.ds(lo, 256), :] = nt(eye, w0_v[:, pl.ds(lo, 256)]).astype(BF16)
 
@@ -124,7 +125,7 @@
         picked, days = [], []
         lanes = pl.ds(first * 128, count * 128)
         for i in (2 * half, 2 * half + 1):
-            if first == 0:
+            if first == 0 and i >= 2:
                 loads[LOADED[i]].wait()
             part = jnp.dot(f_v[i], pick_v[:, lanes], preferred_element_type=F32)
             picked.append(part.astype(BF16))
@@ -221,14 +222,11 @@
     send_x(0, 0)
     network(0, 1, 2)
     send_x(0, 1)
+    network(1, 0, 1)
     send_x(0, 2)
-    turn = selector(128, 128, lambda q: (q & 7) * 16 + (q >> 3))
-    network(1, 0, 1)
+    stage_x(0, 0)
     send_x(1, 0)
-    stage_x(0, 0)
     network(1, 1, 2)
-    send_x(1, 1)
-    send_x(1, 2)
     def placed_from(q):
         source = (q * 21846) >> 16
         d, e = (z - (source >> 4)) & 7, (y - (source >> 1)) & 7
@@ -238,6 +236,8 @@
     for t in range(1, len(chunks) + 1):
         if t < len(chunks):
             stage_x(*chunks[t])
+        if t <= 2:
+            send_x(1, t)
         stage_z(*chunks[t - 1])
     for half in range(2):
         stage_y(half)

time: 47 us -> 47.1 us (level)
  no operation moved by 1% of the time
where the time goes in v2:
time: 47.1 us; the launch traced here: 46.7 us
  Pallas kernels  46.1 us (98%)
  between operations  0.66 us (1%)
    pallas_call x1, Pallas kernels, shards(): pl.pallas_call(kernel, out_shape=jax.ShapeDtypeStruct((2, LANES, BLOCK),...  44 us
    pallas_call x1, Pallas kernels, shards(): pl.pallas_call(spread, out_shape=jax.ShapeDtypeStruct((OUT, COLS), BF16),...  2.05 us

profile of v2, /device:TPU:1, one launch (start us, length us, event | category | flops | bytes accessed | tf_op | source)
XLA Modules:
  0.0 46.7 jit_solution(12065564601542908848)
XLA Ops:
  0.7 44.0 %shard_map.91.t_ref = bf16[2,384,384]{2,1,0:T(8,128)(2,1)} custom-call(s32[1]{0:T(128)S(6)} %copy.10.count_ref, s32[1536]{0:T(1024)} %list_ref.1, bf16[557,1536]{1,0:T(8,128)(2,1)} %feat_ref.1, bf16[557,512]{1,0:T(8,128)(2,1)} %w0_ref.1, f32[512]{0:T(512)} %b0_ref.1, bf16[2,512,512]{2,1,0:T(8,128)(2,1)} %wm_ref.1, f32[2,512]{1,0:T(2,128)} %bm_ref.1, ...), custom_call_target="tpu_custom_call" | custom-call | tf_op jit(solution)/shard_map/pallas_call | solution.py:283
  44.7 2.0 %shard_map.92 = bf16[368,1536]{1,0:T(8,128)(2,1)} custom-call(bf16[2,384,384]{2,1,0:T(8,128)(2,1)} %shard_map.91.t_ref), custom_call_target="tpu_custom_call" | custom-call | tf_op jit(solution)/shard_map/pallas_call | solution.py:331

commit v3 on v2

--- a/solution.py
+++ b/solution.py
@@ -87,11 +87,17 @@
     peers += [(blk, a) for a in sectors[:3]]
     peers += [(along_z[d], x) for d in RING]
     peers += [(along_y[d], x) for d in RING]
-    def picked_from(q):
-        zz, yy = ((q >> 3) + z) & 7, (q + y) & 7
-        return (zz * NY + yy) * (NC * NK) + (((q >> 6) & 1) ^ c) * NK + (q >> 7)
-
-    pick_v[...] = selector(BLOCK, BLOCK, picked_from)
+    def picked_from(half):
+        def source(q):
+            major, minor = (q >> 3) & 7, q & 7
+            z_first = (((q >> 7) + half) & 1) == 0
+            zz = (jnp.where(z_first, major, minor) + z) & 7
+            yy = (jnp.where(z_first, minor, major) + y) & 7
+            return (zz * NY + yy) * (NC * NK) + (((q >> 6) & 1) ^ c) * NK + (q >> 7)
+
+        return source
+
+    pick_v[0] = selector(BLOCK, BLOCK, picked_from(0))
     wo_v[pl.ds(OUT, LANES - OUT), :] = jnp.zeros((LANES - OUT, HID), BF16)
 
     eye = selector(256, 256, lambda r: r)
@@ -127,13 +133,13 @@
         for i in (2 * half, 2 * half + 1):
             if first == 0 and i >= 2:
                 loads[LOADED[i]].wait()
-            part = jnp.dot(f_v[i], pick_v[:, lanes], preferred_element_type=F32)
+            part = jnp.dot(f_v[i], pick_v[half, :, lanes], preferred_element_type=F32)
             picked.append(part.astype(BF16))
             day = jnp.concatenate(
                 [day_v[pl.ds(sectors[i] * NK + t, 1), :] for t in range(NK)], axis=1
             )
             day = jnp.broadcast_to(jnp.where(day > 0.5, 1.0, 0.0), (16, BLOCK)).astype(BF16)
-            days.append(jnp.dot(day, pick_v[:, lanes], preferred_element_type=F32)[:1])
+            days.append(jnp.dot(day, pick_v[half, :, lanes], preferred_element_type=F32)[:1])
         h, day = jnp.concatenate(picked, axis=1), jnp.concatenate(days, axis=1)
         tiled = [jnp.concatenate([b] * (2 * count), axis=1) for b in biases]
         h = jnp.dot(w0t_v[...], h, preferred_element_type=F32)
@@ -172,6 +178,9 @@
     def wait_for(view, sem):
         pltpu.make_async_copy(view, view, sem).wait()
 
+    def axes_of(half, k):
+        return (along_z, along_y) if (half + k) % 2 == 0 else (along_y, along_z)
+
     def stage_x(half, k):
         slots = (0, 1, 2, 3) if half == 0 else (0, 1, 3)
         wait_for(rx.at[half, k, pl.ds(0, len(slots))], rx_sem.at[half, k])
@@ -184,7 +193,7 @@
         zs[half, k] = merged
         for d in RING:
             dst = zr.at[half, k, d]
-            send(zs.at[half, k, d], dst, zs_sem.at[0], zr_sem.at[half, k], (along_z[d], x))
+            send(zs.at[half, k, d], dst, zs_sem.at[0], zr_sem.at[half, k], (axes_of(half, k)[0][d], x))
         zr[half, k, 0] = merged[0]
 
     def stage_z(half, k):
@@ -195,7 +204,7 @@
         ys[half, k] = turned
         for e in RING:
             dst = yr.at[half, k, e]
-            send(ys.at[half, k, e], dst, ys_sem.at[0], yr_sem.at[half, k], (along_y[e], x))
+            send(ys.at[half, k, e], dst, ys_sem.at[0], yr_sem.at[half, k], (axes_of(half, k)[1][e], x))
         yr[half, k, 0] = turned[0]
 
     def stage_y(half):
@@ -210,7 +219,7 @@
             ]
             total = total + jnp.dot(
                 jnp.concatenate(feats, axis=0),
-                place_v[pl.ds(k * 128, 128), :],
+                place_v[half, pl.ds(k * 128, 128), :],
                 preferred_element_type=F32,
             )
         t_v[half] = total.astype(BF16)
@@ -222,17 +231,25 @@
     send_x(0, 0)
     network(0, 1, 2)
     send_x(0, 1)
+    pick_v[1] = selector(BLOCK, BLOCK, picked_from(1))
     network(1, 0, 1)
     send_x(0, 2)
     stage_x(0, 0)
     send_x(1, 0)
     network(1, 1, 2)
-    def placed_from(q):
-        source = (q * 21846) >> 16
-        d, e = (z - (source >> 4)) & 7, (y - (source >> 1)) & 7
-        return (q - source * NK) * 128 + e * 16 + d * 2 + ((source & 1) ^ c)
-
-    place_v[...] = selector(BLOCK, BLOCK, placed_from)
+    def placed_from(half):
+        def row(q):
+            source = (q * 21846) >> 16
+            k = q - source * NK
+            d, e = (z - (source >> 4)) & 7, (y - (source >> 1)) & 7
+            z_first = ((k + half) & 1) == 0
+            major, minor = jnp.where(z_first, e, d), jnp.where(z_first, d, e)
+            return k * 128 + major * 16 + minor * 2 + ((source & 1) ^ c)
+
+        return row
+
+    for half in range(2):
+        place_v[half] = selector(BLOCK, BLOCK, placed_from(half))
     for t in range(1, len(chunks) + 1):
         if t < len(chunks):
             stage_x(*chunks[t])
@@ -296,8 +313,8 @@
             pltpu.VMEM((OUT,), F32),
             pltpu.VMEM((16, 128), F32),
             pltpu.VMEM((HID, FEAT), BF16),
-            pltpu.VMEM((BLOCK, BLOCK), BF16),
-            pltpu.VMEM((BLOCK, BLOCK), BF16),
+            pltpu.VMEM((2, BLOCK, BLOCK), BF16),
+            pltpu.VMEM((2, BLOCK, BLOCK), BF16),
             pltpu.VMEM((NX, NK, NC, ROWS, LANES), BF16),
             pltpu.VMEM((2, NK, 4, ROWS, LANES), BF16),
             pltpu.VMEM((2, NK, NZ, 16, LANES), BF16),

time: 47.1 us -> 46.9 us (level)
  no operation moved by 1% of the time
where the time goes in v3:
time: 46.9 us; the launch traced here: 46.6 us
  Pallas kernels  45.9 us (98%)
  between operations  0.66 us (1%)
    pallas_call x1, Pallas kernels, shards(): pl.pallas_call(kernel, out_shape=jax.ShapeDtypeStruct((2, LANES, BLOCK),...  43.9 us
    pallas_call x1, Pallas kernels, shards(): pl.pallas_call(spread, out_shape=jax.ShapeDtypeStruct((OUT, COLS), BF16),...  2.05 us

profile of v3, /device:TPU:1, one launch (start us, length us, event | category | flops | bytes accessed | tf_op | source)
XLA Modules:
  0.0 46.6 jit_solution(5247879592053622636)
XLA Ops:
  0.7 43.9 %shard_map.91.t_ref = bf16[2,384,384]{2,1,0:T(8,128)(2,1)} custom-call(s32[1]{0:T(128)S(6)} %copy.10.count_ref, s32[1536]{0:T(1024)} %list_ref.1, bf16[557,1536]{1,0:T(8,128)(2,1)} %feat_ref.1, bf16[557,512]{1,0:T(8,128)(2,1)} %w0_ref.1, f32[512]{0:T(512)} %b0_ref.1, bf16[2,512,512]{2,1,0:T(8,128)(2,1)} %wm_ref.1, f32[2,512]{1,0:T(2,128)} %bm_ref.1, ...), custom_call_target="tpu_custom_call" | custom-call | tf_op jit(solution)/shard_map/pallas_call | solution.py:300
  44.6 2.0 %shard_map.92 = bf16[368,1536]{1,0:T(8,128)(2,1)} custom-call(bf16[2,384,384]{2,1,0:T(8,128)(2,1)} %shard_map.91.t_ref), custom_call_target="tpu_custom_call" | custom-call | tf_op jit(solution)/shard_map/pallas_call | solution.py:348

commit v4 on v2

--- a/solution.py
+++ b/solution.py
@@ -80,7 +80,7 @@
 
     barrier = pltpu.get_barrier_semaphore()
     other = blk_of(z, y, 1 - c)
-    cores = (blk, other)
+    core_0, core_1 = blk_of(z, y, 0), blk_of(z, y, 1)
     along_z = [blk_of(lax.rem(z + d, NZ), y, c) for d in range(NZ)]
     along_y = [blk_of(z, lax.rem(y + d, NY), c) for d in range(NY)]
     peers = [(other, a) for a in sectors]
@@ -164,9 +164,9 @@
 
     def send_x(half, k):
         for i in (2 * half, 2 * half + 1):
-            for r in range(NC) if i < 3 else (1,):
+            for r, core in ((c, core_0), (1 - c, core_1)) if i < 3 else ((1, other),):
                 dst = rx.at[half, k, 2 * (i % 2) + r]
-                device = (cores[r], sectors[i])
+                device = (core, sectors[i])
                 send(sx.at[i, k, r], dst, sx_sem.at[0], rx_sem.at[half, k], device)
 
     def wait_for(view, sem):

time: 47.1 us -> 47.5 us (level)
  Pallas kernels: 46.1 us -> 46.6 us
    pallas_call x1, Pallas kernels: 44 us -> 44.6 us  [shards(): pl.pallas_call(kernel, out_shape=jax.ShapeDtypeStruct((2, LANES, BLOCK),...]
where the time goes in v4:
time: 47.5 us; the launch traced here: 47.3 us
  Pallas kernels  46.6 us (98%)
  between operations  0.66 us (1%)
    pallas_call x1, Pallas kernels, shards(): pl.pallas_call(kernel, out_shape=jax.ShapeDtypeStruct((2, LANES, BLOCK),...  44.6 us
    pallas_call x1, Pallas kernels, shards(): pl.pallas_call(spread, out_shape=jax.ShapeDtypeStruct((OUT, COLS), BF16),...  2.05 us

profile of v4, /device:TPU:1, one launch (start us, length us, event | category | flops | bytes accessed | tf_op | source)
XLA Modules:
  0.0 47.3 jit_solution(15609645155340579707)
XLA Ops:
  0.7 44.6 %shard_map.91.t_ref = bf16[2,384,384]{2,1,0:T(8,128)(2,1)} custom-call(s32[1]{0:T(128)S(6)} %copy.10.count_ref, s32[1536]{0:T(1024)} %list_ref.1, bf16[557,1536]{1,0:T(8,128)(2,1)} %feat_ref.1, bf16[557,512]{1,0:T(8,128)(2,1)} %w0_ref.1, f32[512]{0:T(512)} %b0_ref.1, bf16[2,512,512]{2,1,0:T(8,128)(2,1)} %wm_ref.1, f32[2,512]{1,0:T(2,128)} %bm_ref.1, ...), custom_call_target="tpu_custom_call" | custom-call | tf_op jit(solution)/shard_map/pallas_call | solution.py:283
  45.2 2.0 %shard_map.92 = bf16[368,1536]{1,0:T(8,128)(2,1)} custom-call(bf16[2,384,384]{2,1,0:T(8,128)(2,1)} %shard_map.91.t_ref), custom_call_target="tpu_custom_call" | custom-call | tf_op jit(solution)/shard_map/pallas_call | solution.py:331

commit v5 on v2

--- a/solution.py
+++ b/solution.py
@@ -83,13 +83,18 @@
     cores = (blk, other)
     along_z = [blk_of(lax.rem(z + d, NZ), y, c) for d in range(NZ)]
     along_y = [blk_of(z, lax.rem(y + d, NY), c) for d in range(NY)]
+    first_axis = [along_z[d] * (1 - c) + along_y[d] * c for d in range(NZ)]
+    second_axis = [along_y[d] * (1 - c) + along_z[d] * c for d in range(NZ)]
     peers = [(other, a) for a in sectors]
     peers += [(blk, a) for a in sectors[:3]]
     peers += [(along_z[d], x) for d in RING]
     peers += [(along_y[d], x) for d in RING]
     def picked_from(q):
-        zz, yy = ((q >> 3) + z) & 7, (q + y) & 7
-        return (zz * NY + yy) * (NC * NK) + (((q >> 6) & 1) ^ c) * NK + (q >> 7)
+        core = ((q >> 6) & 1) ^ c
+        major, minor = (q >> 3) & 7, q & 7
+        zz = (major * (1 - core) + minor * core + z) & 7
+        yy = (minor * (1 - core) + major * core + y) & 7
+        return (zz * NY + yy) * (NC * NK) + core * NK + (q >> 7)
 
     pick_v[...] = selector(BLOCK, BLOCK, picked_from)
     wo_v[pl.ds(OUT, LANES - OUT), :] = jnp.zeros((LANES - OUT, HID), BF16)
@@ -184,7 +189,7 @@
         zs[half, k] = merged
         for d in RING:
             dst = zr.at[half, k, d]
-            send(zs.at[half, k, d], dst, zs_sem.at[0], zr_sem.at[half, k], (along_z[d], x))
+            send(zs.at[half, k, d], dst, zs_sem.at[0], zr_sem.at[half, k], (first_axis[d], x))
         zr[half, k, 0] = merged[0]
 
     def stage_z(half, k):
@@ -195,7 +200,7 @@
         ys[half, k] = turned
         for e in RING:
             dst = yr.at[half, k, e]
-            send(ys.at[half, k, e], dst, ys_sem.at[0], yr_sem.at[half, k], (along_y[e], x))
+            send(ys.at[half, k, e], dst, ys_sem.at[0], yr_sem.at[half, k], (second_axis[e], x))
         yr[half, k, 0] = turned[0]
 
     def stage_y(half):
@@ -230,7 +235,8 @@
     def placed_from(q):
         source = (q * 21846) >> 16
         d, e = (z - (source >> 4)) & 7, (y - (source >> 1)) & 7
-        return (q - source * NK) * 128 + e * 16 + d * 2 + ((source & 1) ^ c)
+        major, minor = e * (1 - c) + d * c, d * (1 - c) + e * c
+        return (q - source * NK) * 128 + major * 16 + minor * 2 + ((source & 1) ^ c)
 
     place_v[...] = selector(BLOCK, BLOCK, placed_from)
     for t in range(1, len(chunks) + 1):

time: 47.1 us -> 47 us (level)
  the two profiles are of different devices: /device:TPU:1 before, /device:TPU:2 now
where the time goes in v5:
time: 47 us; the launch traced here: 46.9 us
  Pallas kernels  46.2 us (98%)
  between operations  0.66 us (1%)
    pallas_call x1, Pallas kernels, shards(): pl.pallas_call(kernel, out_shape=jax.ShapeDtypeStruct((2, LANES, BLOCK),...  44.2 us
    pallas_call x1, Pallas kernels, shards(): pl.pallas_call(spread, out_shape=jax.ShapeDtypeStruct((OUT, COLS), BF16),...  2.05 us

profile of v5, /device:TPU:2, one launch (start us, length us, event | category | flops | bytes accessed | tf_op | source)
XLA Modules:
  0.0 46.9 jit_solution(6617911618191632519)
XLA Ops:
  0.7 44.2 %shard_map.91.t_ref = bf16[2,384,384]{2,1,0:T(8,128)(2,1)} custom-call(s32[1]{0:T(128)S(6)} %copy.10.count_ref, s32[1536]{0:T(1024)} %list_ref.1, bf16[557,1536]{1,0:T(8,128)(2,1)} %feat_ref.1, bf16[557,512]{1,0:T(8,128)(2,1)} %w0_ref.1, f32[512]{0:T(512)} %b0_ref.1, bf16[2,512,512]{2,1,0:T(8,128)(2,1)} %wm_ref.1, f32[2,512]{1,0:T(2,128)} %bm_ref.1, ...), custom_call_target="tpu_custom_call" | custom-call | tf_op jit(solution)/shard_map/pallas_call | solution.py:289
  44.8 2.0 %shard_map.92 = bf16[368,1536]{1,0:T(8,128)(2,1)} custom-call(bf16[2,384,384]{2,1,0:T(8,128)(2,1)} %shard_map.91.t_ref), custom_call_target="tpu_custom_call" | custom-call | tf_op jit(solution)/shard_map/pallas_call | solution.py:337
